TPU v7x, 512 devices: a whole 4x8x8 slice. The times are simulated.
512 devices in a mesh: ctx: 64 (over x, z, core), head: 8 (over y).
Axes of the slice: x: 4, y: 8, z: 8, core: 2. Of those that a mesh axis runs over, the one named last changes fastest.
Arguments:
- queries: bfloat16 [16384, 64, 128], P('ctx', 'head'), may hold values from -5 to 5
- keys: bfloat16 [16384, 64, 128], P('ctx', 'head'), may hold values from -5 to 5
- values: bfloat16 [16384, 64, 128], P('ctx', 'head'), may hold values from -6 to 6
- selected: int32 [64, 3], P('ctx'), may hold values from 0 to 62, as said below
Outputs:
- attended: bfloat16 [16384, 8192], P(('ctx', 'head'))
Inputs may be any that keep to these rules, and one draw needn't show every extreme that they name: Row q of selected names 3 key blocks for query block q. For q >= 1 it names block q - 1, and its other entries are distinct blocks below q; where fewer than 3 blocks lie below q, the remaining entries equal q and add nothing. Some blocks are named by far more rows than others.
All inputs are finite; a program needn't handle non-finite values.
Results may differ from a plain program's by a relative error of at most 0.0045.
Values may be sent and summed in bfloat16 or wider, within the bound.
A program may use at most 64 MiB of HBM per device.

v0:
```python
import jax
import jax.numpy as jnp
from jax import lax
from jax.sharding import PartitionSpec as P

HEAD_DIM = 128
HEAD_DEV = 8
BLOCK = 256
TOPK = 3


masked_fill = -1e30


def fetch_picked(spread_keys, spread_values, want_index):
    send_keys = jnp.take(spread_keys, want_index, axis=0)
    send_values = jnp.take(spread_values, want_index, axis=0)
    return (
        lax.all_to_all(send_keys, "ctx", split_axis=1, concat_axis=1, tiled=True),
        lax.all_to_all(send_values, "ctx", split_axis=1, concat_axis=1, tiled=True),
    )


def on_device(queries, keys, values, selected):
    ctx_count = lax.axis_size("ctx")
    tok_here = queries.shape[0]
    blocks_here = tok_here // BLOCK
    feat_width = HEAD_DEV * HEAD_DIM
    piece_rows = BLOCK // ctx_count
    score_scale = HEAD_DIM ** (-0.5)
    first_block = lax.axis_index("ctx") * blocks_here
    rows_pos = lax.broadcasted_iota(jnp.int32, (BLOCK, BLOCK), 0)
    cols_pos = lax.broadcasted_iota(jnp.int32, (BLOCK, BLOCK), 1)
    causal = cols_pos <= rows_pos
    local_keys = keys.reshape(blocks_here, ctx_count, piece_rows, feat_width)
    local_values = values.reshape(blocks_here, ctx_count, piece_rows, feat_width)
    spread_keys, spread_values = (
        lax.all_to_all(local_keys, "ctx", split_axis=1, concat_axis=0, tiled=True),
        lax.all_to_all(local_values, "ctx", split_axis=1, concat_axis=0, tiled=True),
    )
    spread_keys = spread_keys.reshape(ctx_count * blocks_here, piece_rows, feat_width)
    spread_values = spread_values.reshape(ctx_count * blocks_here, piece_rows, feat_width)
    chosen = lax.all_gather(selected, "ctx", axis=0, tiled=True)
    want_index = chosen.T
    results = {}
    picked_keys, picked_values = fetch_picked(spread_keys, spread_values, want_index)
    picked_keys = picked_keys.reshape(blocks_here, TOPK, BLOCK, feat_width)
    picked_values = picked_values.reshape(blocks_here, TOPK, BLOCK, feat_width)
    block_at = 0
    for head_at in range(HEAD_DEV):
        cols = slice(head_at * HEAD_DIM, (head_at + 1) * HEAD_DIM)
        far_keys = picked_keys[block_at, :, :, cols]
        far_values = picked_values[block_at, :, :, cols]
        own_id = first_block + block_at
        live_slots = selected[block_at] != own_id
        query_rows = queries[block_at * BLOCK : (block_at + 1) * BLOCK, head_at, :]
        key_rows = keys[block_at * BLOCK : (block_at + 1) * BLOCK, head_at, :]
        raw = lax.dot_general(
            query_rows, key_rows, (((1,), (1,)), ((), ())), preferred_element_type=jnp.float32
        )
        s_own = jnp.where(causal, raw * score_scale, masked_fill)
        attend_query_rows = queries[block_at * BLOCK : (block_at + 1) * BLOCK, head_at, :]
        s_far = (
            jnp.einsum(
                "qd,skd->qsk", attend_query_rows, far_keys, preferred_element_type=jnp.float32
            )
            * score_scale
        )
        s_far = jnp.where(live_slots[None, :, None], s_far, masked_fill).reshape(
            BLOCK, TOPK * BLOCK
        )
        s_all = jnp.concatenate([s_own, s_far], 1)
        allowed = s_all > 0.5 * masked_fill
        row_max = jnp.max(s_all, axis=1, keepdims=True)
        weights = jnp.where(allowed, jnp.exp(s_all - row_max), 0.0)
        totals = jnp.sum(weights, axis=1, keepdims=True)
        rounded = weights.astype(jnp.bfloat16)
        own_values = values[block_at * BLOCK : (block_at + 1) * BLOCK, head_at, :]
        mixed = jnp.dot(rounded[:, :BLOCK], own_values, preferred_element_type=jnp.float32)
        mixed = mixed + jnp.dot(
            rounded[:, BLOCK:],
            far_values.reshape(TOPK * BLOCK, HEAD_DIM),
            preferred_element_type=jnp.float32,
        )
        results[block_at, head_at] = (mixed / totals).astype(jnp.bfloat16)
    block_at = 0
    stacked = jnp.stack([results[block_at, head_at] for head_at in range(HEAD_DEV)], axis=1)
    block_rows = stacked.reshape(BLOCK, feat_width)
    return lax.all_to_all(block_rows, "head", split_axis=0, concat_axis=1, tiled=True)


def solution(mesh):
    return jax.shard_map(
        on_device,
        mesh=mesh,
        in_specs=(
            P("ctx", "head", None),
            P("ctx", "head", None),
            P("ctx", "head", None),
            P("ctx", None),
        ),
        out_specs=P(("ctx", "head"), None),
        check_vma=False,
    )
```

profile of v0, /device:TPU:1, one launch (start us, length us, event | category | flops | bytes accessed | tf_op | source)
XLA Modules:
  0.0 228.2 jit_solution(16346284471922282913)
XLA Ops:
  0.0 2.0 reshape.119
  2.0 15.0 %all-to-all-start.2 = ((bf16[1,64,4,1024]{3,2,0,1:T(4,128)(2,1)}), bf16[1,64,4,1024]{3,2,0,1:T(4,128)(2,1)S(1)}, u32[]{:S(2)}, u32[]{:S(2)}) async-start(bf16[1,64,4,1024]{3,2,0,1:T(4,128)(2,1)} %reshape.119), calls=%async_computation.2 | async-start | bytes 1048576 | tf_op jit(solution)/shard_map/all_to_all | solution.py:39
  17.0 0.9 reshape.115
  17.9 16.4 %all-to-all-done.2 = bf16[1,64,4,1024]{3,2,0,1:T(4,128)(2,1)S(1)} async-done(((bf16[1,64,4,1024]{3,2,0,1:T(4,128)(2,1)}), bf16[1,64,4,1024]{3,2,0,1:T(4,128)(2,1)S(1)}, u32[]{:S(2)}, u32[]{:S(2)}) %all-to-all-start.2) | async-done | bytes 524320 | tf_op jit(solution)/shard_map/all_to_all | solution.py:39
  34.3 6.3 %all-to-all-start = ((bf16[1,64,4,1024]{3,2,0,1:T(4,128)(2,1)}), bf16[1,64,4,1024]{3,2,0,1:T(4,128)(2,1)S(1)}, u32[]{:S(2)}, u32[]{:S(2)}) async-start(bf16[1,64,4,1024]{3,2,0,1:T(4,128)(2,1)} %reshape.115), calls=%async_computation | async-start | bytes 1048576 | tf_op jit(solution)/shard_map/all_to_all | solution.py:38
  40.6 48.3 %all-gather = s32[64,1,3]{2,1,0:T(1,128)S(1)} all-gather(s32[1,1,3]{2,1,0:T(1,128)S(1)} %bitcast.292), channel_id=1, replica_groups=mesh['ctx'=64,'head'=8] {'ctx'}, dimensions={0}, use_global_device_ids=true | all-gather | bytes 780 | tf_op jit(solution)/shard_map/all_gather | solution.py:43
  89.1 1.9 gather_fusion.1
  91.0 3.2 %gather_fusion = bf16[192,4,1024]{2,1,0:T(4,128)(2,1)} fusion(bf16[64,4,1024]{2,1,0:T(4,128)(2,1)S(1)} %bitcast.270, s32[1024]{0:T(1024)S(1)} %pad_clamp_fusion), kind=kCustom, calls=%fused_computation.clone | custom fusion | bytes 3146496 | tf_op jit(solution)/shard_map/jit(_take)/gather | solution.py:16
  94.2 3.9 %copy_select_fusion = (bf16[3,64,4,1024]{3,2,0,1:T(4,128)(2,1)}, bf16[3,64,4,1024]{3,2,0,1:T(4,128)(2,1)}) fusion(bf16[3,64,4,1024]{3,2,1,0:T(4,128)(2,1)S(1)} %bitcast.271, pred[3,64]{0,1:T(8,128)(4,1)S(1)} %compare_and_fusion, bf16[3,64,4,1024]{3,2,1,0:T(4,128)(2,1)} %bitcast.272), kind=kLoop, calls=%fused_computation.2 | loop fusion | flops 1572864 | bytes 6291648 | tf_op jit(solution)/shard_map/jit(_take)/select_n | solution.py:17
  98.1 5.4 %all-to-all-start.1 = ((bf16[3,64,4,1024]{3,2,0,1:T(4,128)(2,1)}), bf16[3,64,4,1024]{3,2,0,1:T(4,128)(2,1)S(1)}, u32[]{:S(2)}, u32[]{:S(2)}) async-start(bf16[3,64,4,1024]{3,2,0,1:T(4,128)(2,1)} %get-tuple-element.55), calls=%async_computation.1 | async-start | bytes 3145728 | tf_op jit(solution)/shard_map/all_to_all | solution.py:19
  103.5 1.5 fusion.122
  105.0 0.9 fusion.123
  106.1 1.5 fusion.124
  107.6 1.4 fusion.126
  109.0 1.4 fusion.128
  110.4 1.4 fusion.130
  111.9 1.4 fusion.132
  113.3 30.0 %all-to-all-done.1 = bf16[3,64,4,1024]{3,2,0,1:T(4,128)(2,1)S(1)} async-done(((bf16[3,64,4,1024]{3,2,0,1:T(4,128)(2,1)}), bf16[3,64,4,1024]{3,2,0,1:T(4,128)(2,1)S(1)}, u32[]{:S(2)}, u32[]{:S(2)}) %all-to-all-start.1) | async-done | bytes 1572896 | tf_op jit(solution)/shard_map/all_to_all | solution.py:19
  143.3 6.1 %all-to-all-start.3 = ((bf16[3,64,4,1024]{3,2,0,1:T(4,128)(2,1)}), bf16[3,64,4,1024]{3,2,0,1:T(4,128)(2,1)S(1)}, u32[]{:S(2)}, u32[]{:S(2)}) async-start(bf16[3,64,4,1024]{3,2,0,1:T(4,128)(2,1)} %get-tuple-element.54), calls=%async_computation.3 | async-start | bytes 3145728 | tf_op jit(solution)/shard_map/all_to_all | solution.py:20
  149.5 2.5 %fusion.134 = (f32[256]{0:T(256)}, f32[256,256]{0,1:T(8,128)}) fusion(bf16[256,1,128]{2,1,0:T(2,128)(2,1)} %get-tuple-element.40, bf16[256,1,128]{2,1,0:T(2,128)(2,1)S(1)} %get-tuple-element.48), kind=kOutput, calls=%fused_computation.207 | convolution fusion | flops 17039104 | bytes 394240 | tf_op jit(solution)/shard_map/dot_general | solution.py:58
  152.0 2.4 %fusion.136 = (f32[256]{0:T(256)}, f32[256,256]{0,1:T(8,128)}) fusion(bf16[256,1,128]{2,1,0:T(2,128)(2,1)} %get-tuple-element.39, bf16[256,1,128]{2,1,0:T(2,128)(2,1)S(1)} %get-tuple-element.47), kind=kOutput, calls=%fused_computation.209 | convolution fusion | flops 17039104 | bytes 394240 | tf_op jit(solution)/shard_map/dot_general | solution.py:58
  154.4 2.3 %fusion.138 = (f32[256]{0:T(256)}, f32[256,256]{0,1:T(8,128)}) fusion(bf16[256,1,128]{2,1,0:T(2,128)(2,1)} %get-tuple-element.38, bf16[256,1,128]{2,1,0:T(2,128)(2,1)S(1)} %get-tuple-element.46), kind=kOutput, calls=%fused_computation.211 | convolution fusion | flops 17039104 | bytes 394240 | tf_op jit(solution)/shard_map/dot_general | solution.py:58
  156.7 1.6 fusion.121
  158.3 1.7 copy.109
  160.0 2.4 %reshape.117 = bf16[1,3,256,1024]{3,2,1,0:T(8,128)(2,1)S(1)} reshape(bf16[3,64,4,1024]{3,2,1,0:T(4,128)(2,1)} %copy.109) | data formatting | bytes 3145728 | tf_op jit(solution)/shard_map/reshape | solution.py:47
  162.4 2.6 %fusion.125 = (f32[256]{0:T(256)}, f32[3,256,256]{2,1,0:T(8,128)}) fusion(bf16[256,1,128]{2,1,0:T(2,128)(2,1)} %copy-done.29, bf16[1,3,256,1024]{3,2,1,0:T(8,128)(2,1)S(1)} %reshape.117, pred[3]{0:T(512)(128)(4,1)S(1)} %compare_bitcast_fusion), kind=kOutput, calls=%fused_computation.198 | convolution fusion | flops 50921216 | bytes 1050112 | tf_op jit(solution)/shard_map/qd,skd->qsk/dot_general | solution.py:64
  165.0 2.7 %fusion.127 = (f32[256]{0:T(256)}, f32[3,256,256]{2,1,0:T(8,128)}) fusion(bf16[256,1,128]{2,1,0:T(2,128)(2,1)} %copy-done.28, bf16[1,3,256,1024]{3,2,1,0:T(8,128)(2,1)S(1)} %reshape.117, pred[3]{0:T(512)(128)(4,1)S(1)} %compare_bitcast_fusion), kind=kOutput, calls=%fused_computation.200 | convolution fusion | flops 50921216 | bytes 1050112 | tf_op jit(solution)/shard_map/qd,skd->qsk/dot_general | solution.py:64
  167.7 1.7 fusion.129
  169.4 1.8 fusion.131
  171.1 1.7 fusion.133
  172.9 1.2 fusion.135
  174.1 1.2 fusion.137
  175.2 1.2 fusion.139
  176.4 12.9 %all-to-all-done.3 = bf16[3,64,4,1024]{3,2,0,1:T(4,128)(2,1)S(1)} async-done(((bf16[3,64,4,1024]{3,2,0,1:T(4,128)(2,1)}), bf16[3,64,4,1024]{3,2,0,1:T(4,128)(2,1)S(1)}, u32[]{:S(2)}, u32[]{:S(2)}) %all-to-all-start.3) | async-done | bytes 1572896 | tf_op jit(solution)/shard_map/all_to_all | solution.py:20
  189.3 1.7 copy.113
  191.0 2.4 %reshape.121 = bf16[1,3,256,1024]{3,2,1,0:T(8,128)(2,1)S(1)} reshape(bf16[3,64,4,1024]{3,2,1,0:T(4,128)(2,1)} %copy.113) | data formatting | bytes 3145728 | tf_op jit(solution)/shard_map/reshape | solution.py:48
  193.4 0.4 fusion.120
  194.0 0.5 copy-done.9
  199.8 0.3 fusion.45
  200.2 0.3 fusion.43
  200.5 0.3 fusion.41
  200.9 0.3 fusion.39
  201.2 0.3 fusion.37
  201.6 0.3 fusion.35
  201.9 0.3 fusion.33
  202.2 0.3 copy.135
  202.8 24.5 %all_to_all.47 = bf16[8,32,1024]{2,1,0:T(8,128)(2,1)S(1)} all-to-all(bf16[8,32,1024]{2,1,0:T(8,128)(2,1)S(1)} %all_to_all.38), channel_id=1, replica_groups=mesh['ctx'=64,'head'=8] {'head'}, dimensions={0} | all-to-all | bytes 1048576 | tf_op jit(solution)/shard_map/all_to_all | solution.py:89
  227.3 0.8 copy.161
  (136 shorter events, 5.7 us)
Async XLA Ops:
  0.0 17.0 %copy-start = (bf16[256,8,128]{2,1,0:T(8,128)(2,1)S(1)}, bf16[256,8,128]{2,1,0:T(8,128)(2,1)}, u32[]{:S(2)}) copy-start(bf16[256,8,128]{2,1,0:T(8,128)(2,1)} %param.7) | copy-start | bytes 1572868
  2.0 38.6 %copy-start.51 = (s32[1,3]{1,0:T(1,128)S(1)}, s32[1,3]{1,0:T(1,128)}, u32[]{:S(2)}) copy-start(s32[1,3]{1,0:T(1,128)} %param.9) | copy-start | bytes 40
  2.0 32.3 %all-to-all-start.2 = ((bf16[1,64,4,1024]{3,2,0,1:T(4,128)(2,1)}), bf16[1,64,4,1024]{3,2,0,1:T(4,128)(2,1)S(1)}, u32[]{:S(2)}, u32[]{:S(2)}) async-start(bf16[1,64,4,1024]{3,2,0,1:T(4,128)(2,1)} %reshape.119), calls=%async_computation.2 | async-start | bytes 1048576 | tf_op jit(solution)/shard_map/all_to_all | solution.py:39
  34.3 56.7 %all-to-all-start = ((bf16[1,64,4,1024]{3,2,0,1:T(4,128)(2,1)}), bf16[1,64,4,1024]{3,2,0,1:T(4,128)(2,1)S(1)}, u32[]{:S(2)}, u32[]{:S(2)}) async-start(bf16[1,64,4,1024]{3,2,0,1:T(4,128)(2,1)} %reshape.115), calls=%async_computation | async-start | bytes 1048576 | tf_op jit(solution)/shard_map/all_to_all | solution.py:38
  98.1 45.2 %all-to-all-start.1 = ((bf16[3,64,4,1024]{3,2,0,1:T(4,128)(2,1)}), bf16[3,64,4,1024]{3,2,0,1:T(4,128)(2,1)S(1)}, u32[]{:S(2)}, u32[]{:S(2)}) async-start(bf16[3,64,4,1024]{3,2,0,1:T(4,128)(2,1)} %get-tuple-element.55), calls=%async_computation.1 | async-start | bytes 3145728 | tf_op jit(solution)/shard_map/all_to_all | solution.py:19
  103.5 1.5 copy-start.10
  106.0 37.3 %copy-start.21 = (bf16[256,1,128]{2,1,0:T(2,128)(2,1)}, bf16[256,1,128]{2,1,0:T(2,128)(2,1)S(1)}, u32[]{:S(2)}) copy-start(bf16[256,1,128]{2,1,0:T(2,128)(2,1)S(1)} %get-tuple-element.49) | copy-start | bytes 196612
  106.0 37.3 %copy-start.23 = (bf16[256,1,128]{2,1,0:T(2,128)(2,1)}, bf16[256,1,128]{2,1,0:T(2,128)(2,1)S(1)}, u32[]{:S(2)}) copy-start(bf16[256,1,128]{2,1,0:T(2,128)(2,1)S(1)} %get-tuple-element.50) | copy-start | bytes 196612
  106.0 37.3 %copy-start.26 = (bf16[256,1,128]{2,1,0:T(2,128)(2,1)}, bf16[256,1,128]{2,1,0:T(2,128)(2,1)S(1)}, u32[]{:S(2)}) copy-start(bf16[256,1,128]{2,1,0:T(2,128)(2,1)S(1)} %get-tuple-element.51) | copy-start | bytes 196612
  106.0 37.3 %copy-start.28 = (bf16[256,1,128]{2,1,0:T(2,128)(2,1)}, bf16[256,1,128]{2,1,0:T(2,128)(2,1)S(1)}, u32[]{:S(2)}) copy-start(bf16[256,1,128]{2,1,0:T(2,128)(2,1)S(1)} %get-tuple-element.52) | copy-start | bytes 196612
  106.0 37.3 %copy-start.29 = (bf16[256,1,128]{2,1,0:T(2,128)(2,1)}, bf16[256,1,128]{2,1,0:T(2,128)(2,1)S(1)}, u32[]{:S(2)}) copy-start(bf16[256,1,128]{2,1,0:T(2,128)(2,1)S(1)} %get-tuple-element.53) | copy-start | bytes 196612
  106.0 43.5 %copy-start.19 = (bf16[256,1,128]{2,1,0:T(2,128)(2,1)}, bf16[256,1,128]{2,1,0:T(2,128)(2,1)S(1)}, u32[]{:S(2)}) copy-start(bf16[256,1,128]{2,1,0:T(2,128)(2,1)S(1)} %get-tuple-element.48) | copy-start | bytes 196612
  106.0 45.9 %copy-start.17 = (bf16[256,1,128]{2,1,0:T(2,128)(2,1)}, bf16[256,1,128]{2,1,0:T(2,128)(2,1)S(1)}, u32[]{:S(2)}) copy-start(bf16[256,1,128]{2,1,0:T(2,128)(2,1)S(1)} %get-tuple-element.47) | copy-start | bytes 196612
  106.1 48.3 %copy-start.14 = (bf16[256,1,128]{2,1,0:T(2,128)(2,1)}, bf16[256,1,128]{2,1,0:T(2,128)(2,1)S(1)}, u32[]{:S(2)}) copy-start(bf16[256,1,128]{2,1,0:T(2,128)(2,1)S(1)} %get-tuple-element.46) | copy-start | bytes 196612
  143.3 45.9 %all-to-all-start.3 = ((bf16[3,64,4,1024]{3,2,0,1:T(4,128)(2,1)}), bf16[3,64,4,1024]{3,2,0,1:T(4,128)(2,1)S(1)}, u32[]{:S(2)}, u32[]{:S(2)}) async-start(bf16[3,64,4,1024]{3,2,0,1:T(4,128)(2,1)} %get-tuple-element.54), calls=%async_computation.3 | async-start | bytes 3145728 | tf_op jit(solution)/shard_map/all_to_all | solution.py:20
  149.5 7.2 %copy-start.1 = (bf16[256,8,128]{2,1,0:T(8,128)(2,1)S(1)}, bf16[256,8,128]{2,1,0:T(8,128)(2,1)}, u32[]{:S(2)}) copy-start(bf16[256,8,128]{2,1,0:T(8,128)(2,1)} %param.8) | copy-start | bytes 1572868
  162.4 5.3 %copy-start.27 = (bf16[256,1,128]{2,1,0:T(2,128)(2,1)S(1)}, bf16[256,1,128]{2,1,0:T(2,128)(2,1)}, u32[]{:S(2)}) copy-start(bf16[256,1,128]{2,1,0:T(2,128)(2,1)} %copy-done.26) | copy-start | bytes 196612
  162.4 7.0 %copy-start.24 = (bf16[256,1,128]{2,1,0:T(2,128)(2,1)S(1)}, bf16[256,1,128]{2,1,0:T(2,128)(2,1)}, u32[]{:S(2)}) copy-start(bf16[256,1,128]{2,1,0:T(2,128)(2,1)} %copy-done.23) | copy-start | bytes 196612
  165.0 6.1 %copy-start.22 = (bf16[256,1,128]{2,1,0:T(2,128)(2,1)S(1)}, bf16[256,1,128]{2,1,0:T(2,128)(2,1)}, u32[]{:S(2)}) copy-start(bf16[256,1,128]{2,1,0:T(2,128)(2,1)} %copy-done.21) | copy-start | bytes 196612
  167.7 5.2 %copy-start.20 = (bf16[256,1,128]{2,1,0:T(2,128)(2,1)S(1)}, bf16[256,1,128]{2,1,0:T(2,128)(2,1)}, u32[]{:S(2)}) copy-start(bf16[256,1,128]{2,1,0:T(2,128)(2,1)} %copy-done.19) | copy-start | bytes 196612
  169.4 4.7 %copy-start.18 = (bf16[256,1,128]{2,1,0:T(2,128)(2,1)S(1)}, bf16[256,1,128]{2,1,0:T(2,128)(2,1)}, u32[]{:S(2)}) copy-start(bf16[256,1,128]{2,1,0:T(2,128)(2,1)} %copy-done.17) | copy-start | bytes 196612
  171.1 4.1 %copy-start.15 = (bf16[256,1,128]{2,1,0:T(2,128)(2,1)S(1)}, bf16[256,1,128]{2,1,0:T(2,128)(2,1)}, u32[]{:S(2)}) copy-start(bf16[256,1,128]{2,1,0:T(2,128)(2,1)} %copy-done.14) | copy-start | bytes 196612
  193.4 1.1 copy-start.9
  193.4 1.2 copy-start.37
  193.8 1.3 copy-start.41
  193.8 1.3 copy-start.49
  193.8 1.3 copy-start.8
  193.8 1.3 copy-start.36
  194.6 1.2 copy-start.40
  194.6 1.2 copy-start.48
  194.6 1.3 copy-start.7
  194.6 1.3 copy-start.35
  195.1 1.3 copy-start.39
  195.2 1.3 copy-start.47
  195.2 1.3 copy-start.6
  195.2 1.3 copy-start.34
  195.9 1.2 copy-start.38
  195.9 1.2 copy-start.45
  195.9 1.3 copy-start.5
  195.9 1.3 copy-start.32
  196.5 1.2 copy-start.46
  196.5 1.3 copy-start.4
  196.5 1.3 copy-start.33
  197.2 1.2 copy-start.3
  197.2 1.3 copy-start.31
  197.8 1.2 copy-start.43
  197.8 1.2 copy-start.2
  197.8 1.3 copy-start.30
  (8 other events, 7.4 us)
where the time goes:
time: 229 us; the launch traced here: 228 us
  blocking collectives  72.8 us (32%)
  waiting for transfers between devices  59.3 us (26%)
  starting transfers between devices  32.8 us (14%)
  matrix products  32.8 us (14%)
  local copies, waits for them, and re-layouts  23.7 us (10%)
  other arithmetic  6.11 us (3%)
    all_gather x1, blocking collectives, on_device(): chosen = lax.all_gather(selected, 'ctx', axis=0, tiled=True)  48.3 us
    all_to_all x1, waiting for transfers between devices, fetch_picked(): lax.all_to_all(send_keys, 'ctx', split_axis=1, concat_axis=1, tiled=True)  30 us
    all_to_all x1, blocking collectives, on_device(): lax.all_to_all(block_rows, 'head', split_axis=0, concat_axis=1, tiled=True)  24.5 us
    all_to_all x1, waiting for transfers between devices, on_device(): lax.all_to_all(local_values, 'ctx', split_axis=1, concat_axis=0, tiled=True)  16.4 us
    all_to_all x1, starting transfers between devices, on_device(): lax.all_to_all(local_values, 'ctx', split_axis=1, concat_axis=0, tiled=True)  15 us
    dot_general x8, matrix products, on_device(): lax.dot_general(query_rows, key_rows, (((1,), (1,)), ((), ())), preferred...  14.4 us
    dot_general x8, matrix products, on_device(): jnp.einsum('qd,skd->qsk', attend_query_rows, far_keys, preferred_element_...  14 us
    all_to_all x1, waiting for transfers between devices, fetch_picked(): lax.all_to_all(send_values, 'ctx', split_axis=1, concat_axis=1, tiled=True)  12.9 us
  transfers between devices with their start and end apart: 4, of which 3 were waited for; matrix products, arithmetic and copies ran while one was open for 17% of the time, Pallas kernels for 0%

commit v1 on v0

v1 whole, which is shorter than its diff:
```python
import functools
import math

import jax
import jax.numpy as jnp
from jax import lax
from jax.experimental import pallas as pl
from jax.experimental.pallas import tpu as pltpu
from jax.sharding import PartitionSpec as P

HEAD_DIM = 128
BLOCK = 256
CHUNKS = 2
MESH = pl.DeviceIdType.MESH
STRIDE = 27

FILL = -1e30
EXP_SCALE = HEAD_DIM ** (-0.5) * math.log2(math.e)


def kernel(
    n_ctx, n_head, heads,
    sel_ref, q_hbm, k_hbm, v_hbm, out_ref,
    q_ref, k_ref, v_ref, in_sem, q_heads, own, send, far, near, staged, wide,
    sel_own, sel_all, sel_smem,
    sel_send, sel_recv, sel_local, spread_send, spread_recv, fetch_send, fetch_recv,
    near_send, near_recv, out_send, out_recv,
    *spread,
):
    group = heads // CHUNKS
    pieces_of_head = n_ctx // (2 * group)
    me = lax.axis_index("ctx")
    my_head = lax.axis_index("head")
    right = lax.rem(me + 1, n_ctx)
    rows_out = BLOCK // n_head
    cols_out = group * HEAD_DIM

    def to_ctx(i):
        return lax.rem(me + i * STRIDE, n_ctx)

    def to_head(i):
        return lax.rem(my_head + i, n_head)

    loads = [
        pltpu.make_async_copy(src, dst, in_sem.at[i])
        for i, (src, dst) in enumerate([(k_hbm, k_ref), (v_hbm, v_ref), (q_hbm, q_ref)])
    ]
    for load in loads:
        load.start()

    barrier = pltpu.get_barrier_semaphore()

    @pl.loop(1, n_ctx)
    def _(i):
        pl.semaphore_signal(barrier, inc=1, device_id={"ctx": to_ctx(i)}, device_id_type=MESH)

    @pl.loop(1, n_head)
    def _(i):
        pl.semaphore_signal(barrier, inc=1, device_id={"head": to_head(i)}, device_id_type=MESH)

    s0, s1, s2 = sel_ref[0, 0], sel_ref[0, 1], sel_ref[0, 2]
    far_a = jnp.where(s0 == me - 1, s1, s0)
    far_b = jnp.where(s2 == me - 1, s1, s2)
    lane = lax.broadcasted_iota(jnp.int32, (1, 128), 1)
    sel_own[...] = jnp.where(lane == 0, far_a, far_b)

    def split_heads(src, store, first, count):
        wide[...] = src[...].astype(jnp.float32).reshape(BLOCK * heads, HEAD_DIM)
        for h in range(first, first + count):
            store(h, wide[pl.ds(h, BLOCK, stride=heads), :].astype(jnp.bfloat16))

    def store_own(kind):
        def store(h, rows):
            chunk, at = divmod(h, group)
            start = (kind * group + at) * pieces_of_head
            own[chunk, pl.ds(start, pieces_of_head)] = rows.reshape(
                pieces_of_head, BLOCK // pieces_of_head, HEAD_DIM
            )
        return store

    def store_q(h, rows):
        q_heads[h] = rows

    def spread_copy(chunk, peer):
        return pltpu.make_async_remote_copy(
            src_ref=own.at[chunk, peer], dst_ref=spread[chunk].at[me],
            send_sem=spread_send.at[chunk], recv_sem=spread_recv.at[chunk],
            device_id={"ctx": peer}, device_id_type=MESH,
        )

    def near_copy(chunk):
        return pltpu.make_async_remote_copy(
            src_ref=own.at[chunk], dst_ref=near.at[chunk],
            send_sem=near_send.at[chunk], recv_sem=near_recv.at[chunk],
            device_id={"ctx": right}, device_id_type=MESH,
        )

    def sel_copy(peer):
        return pltpu.make_async_remote_copy(
            src_ref=sel_own, dst_ref=sel_all.at[me],
            send_sem=sel_send, recv_sem=sel_recv,
            device_id={"ctx": peer}, device_id_type=MESH,
        )

    def fetch_copy(chunk, peer):
        return pltpu.make_async_remote_copy(
            src_ref=send.at[chunk, peer], dst_ref=far.at[chunk, :, me],
            send_sem=fetch_send.at[chunk], recv_sem=fetch_recv.at[chunk],
            device_id={"ctx": peer}, device_id_type=MESH,
        )

    def out_slot(chunk):
        return out_ref.at[:, pl.ds(pl.multiple_of(my_head * (heads * HEAD_DIM) + chunk * cols_out, HEAD_DIM), cols_out)]

    def out_copy(chunk, peer):
        return pltpu.make_async_remote_copy(
            src_ref=staged.at[chunk, peer], dst_ref=out_slot(chunk),
            send_sem=out_send.at[chunk], recv_sem=out_recv.at[chunk],
            device_id={"head": peer}, device_id_type=MESH,
        )

    def wait_bytes(ref, sem):
        pltpu.make_async_copy(ref, ref, sem).wait()

    loads[0].wait()
    split_heads(k_ref, store_own(0), 0, heads)
    loads[1].wait()
    split_heads(v_ref, store_own(1), 0, heads)

    pl.semaphore_wait(barrier, n_ctx - 1 + n_head - 1)

    pltpu.make_async_copy(sel_own, sel_all.at[me], sel_recv).start()

    @pl.loop(1, n_ctx)
    def _(i):
        sel_copy(to_ctx(i)).start()

    for chunk in range(CHUNKS):
        pltpu.make_async_copy(own.at[chunk, me], spread[chunk].at[me], spread_recv.at[chunk]).start()

        @pl.loop(1, n_ctx)
        def _(i):
            spread_copy(chunk, to_ctx(i)).start()

        near_copy(chunk).start()

    loads[2].wait()
    split_heads(q_ref, store_q, 0, heads)

    wait_bytes(sel_all, sel_recv)
    sel_down = pltpu.make_async_copy(sel_all, sel_smem, sel_local)
    sel_down.start()
    sel_down.wait()

    for chunk in range(CHUNKS):
        wait_bytes(spread[chunk], spread_recv.at[chunk])

        def fill(peer):
            for slot in range(2):
                send[chunk, peer, slot] = spread[chunk][sel_smem[peer, 0, slot]]

        @pl.loop(1, n_ctx)
        def _(i):
            peer = to_ctx(i)
            fill(peer)
            fetch_copy(chunk, peer).start()

        fill(me)
        pltpu.make_async_copy(send.at[chunk, me], far.at[chunk, :, me], fetch_recv.at[chunk]).start()

    causal = lax.broadcasted_iota(jnp.int32, (BLOCK, BLOCK), 1) <= lax.broadcasted_iota(
        jnp.int32, (BLOCK, BLOCK), 0
    )
    near_live, a_live, b_live = me >= 1, far_a != me, far_b != me

    def scores(q, k):
        return lax.dot_general(q, k, (((1,), (1,)), ((), ())), preferred_element_type=jnp.float32)

    def half_max(s):
        return jnp.maximum(s[:, :128], s[:, 128:])

    for chunk in range(CHUNKS):
        wait_bytes(near.at[chunk], near_recv.at[chunk])
        wait_bytes(far.at[chunk], fetch_recv.at[chunk])

        for at in range(group):
            def pick(buf, kind):
                first = (kind * group + at) * pieces_of_head
                return buf[pl.ds(first, pieces_of_head)].reshape(BLOCK, HEAD_DIM)

            blocks = [own.at[chunk], near.at[chunk], far.at[chunk, 0], far.at[chunk, 1]]
            live = [None, near_live, a_live, b_live]
            q = q_heads[chunk * group + at]
            s = [scores(q, pick(b, 0)) for b in blocks]
            s[0] = jnp.where(causal, s[0], FILL)
            top = half_max(s[0])
            for one, ok in zip(s[1:], live[1:]):
                top = jnp.maximum(top, jnp.where(ok, half_max(one), FILL))
            top = jnp.max(top, axis=1, keepdims=True) * EXP_SCALE
            total, mixed = None, None
            for one, ok, b in zip(s, live, blocks):
                shift = top if ok is None else jnp.where(ok, top, -FILL)
                w = jnp.exp2(one * EXP_SCALE - shift)
                part = w[:, :128] + w[:, 128:]
                total = part if total is None else total + part
                part = jnp.dot(w.astype(jnp.bfloat16), pick(b, 1), preferred_element_type=jnp.float32)
                mixed = part if mixed is None else mixed + part
            total = jnp.sum(total, axis=1, keepdims=True)
            rows = (mixed / total).astype(jnp.bfloat16)
            staged[chunk, :, :, at * HEAD_DIM : (at + 1) * HEAD_DIM] = rows.reshape(
                n_head, rows_out, HEAD_DIM
            )

        pltpu.make_async_copy(staged.at[chunk, my_head], out_slot(chunk), out_recv.at[chunk]).start()

        @pl.loop(1, n_head)
        def _(i):
            out_copy(chunk, to_head(i)).start()

    others = pl.ds(0, n_ctx - 1)
    wait_bytes(sel_all.at[others], sel_send)
    for chunk in range(CHUNKS):
        wait_bytes(spread[chunk].at[others], spread_send.at[chunk])
        wait_bytes(send.at[chunk, others], fetch_send.at[chunk])
        wait_bytes(near.at[chunk], near_send.at[chunk])
        wait_bytes(staged.at[chunk, pl.ds(0, n_head - 1)], out_send.at[chunk])
        wait_bytes(staged.at[chunk], out_recv.at[chunk])


def on_device(n_ctx, n_head, selected, queries, keys, values):
    heads = queries.shape[1]
    group = heads // CHUNKS
    piece = 2 * group * BLOCK // n_ctx
    bf16, dma = jnp.bfloat16, pltpu.SemaphoreType.DMA
    hbm = pl.BlockSpec(memory_space=pltpu.HBM)
    return pl.pallas_call(
        functools.partial(kernel, n_ctx, n_head, heads),
        out_shape=jax.ShapeDtypeStruct((BLOCK // n_head, n_head * heads * HEAD_DIM), bf16),
        in_specs=[pl.BlockSpec(memory_space=pltpu.SMEM), hbm, hbm, hbm],
        out_specs=pl.BlockSpec(memory_space=pl.ANY),
        scratch_shapes=[
            *[pltpu.VMEM((BLOCK, heads, HEAD_DIM), bf16)] * 3,
            dma((3,)),
            pltpu.VMEM((heads, BLOCK, HEAD_DIM), bf16),
            pltpu.VMEM((CHUNKS, n_ctx, piece, HEAD_DIM), bf16),
            pltpu.VMEM((CHUNKS, n_ctx, 2, piece, HEAD_DIM), bf16),
            pltpu.VMEM((CHUNKS, 2, n_ctx, piece, HEAD_DIM), bf16),
            pltpu.VMEM((CHUNKS, n_ctx, piece, HEAD_DIM), bf16),
            pltpu.VMEM((CHUNKS, n_head, BLOCK // n_head, group * HEAD_DIM), bf16),
            pltpu.VMEM((BLOCK * heads, HEAD_DIM), jnp.float32),
            pltpu.VMEM((1, 128), jnp.int32),
            pltpu.VMEM((n_ctx, 1, 128), jnp.int32),
            pltpu.SMEM((n_ctx, 1, 128), jnp.int32),
            dma, dma, dma,
            dma((CHUNKS,)), dma((CHUNKS,)),
            dma((CHUNKS,)), dma((CHUNKS,)),
            dma((CHUNKS,)), dma((CHUNKS,)),
            dma((CHUNKS,)), dma((CHUNKS,)),
            *[pltpu.VMEM((n_ctx, piece, HEAD_DIM), bf16)] * CHUNKS,
        ],
        compiler_params=pltpu.CompilerParams(
            collective_id=0, has_side_effects=True, vmem_limit_bytes=63 * 1024 * 1024
        ),
        name="moba",
    )(selected, queries, keys, values)


def solution(mesh):
    n_ctx, n_head = mesh.shape["ctx"], mesh.shape["head"]

    def run(queries, keys, values, selected):
        return on_device(n_ctx, n_head, selected, queries, keys, values)

    return jax.shard_map(
        run,
        mesh=mesh,
        in_specs=(
            P("ctx", "head", None),
            P("ctx", "head", None),
            P("ctx", "head", None),
            P("ctx", None),
        ),
        out_specs=P(("ctx", "head"), None),
        check_vma=False,
    )
```

time: 229 us -> 112 us (0.49)
  Pallas kernels: 0 us -> 110 us
  blocking collectives: 72.8 us -> 0 us
  waiting for transfers between devices: 59.3 us -> 0 us
  matrix products: 32.8 us -> 0 us
  starting transfers between devices: 32.8 us -> 0 us
  local copies, waits for them, and re-layouts: 23.7 us -> 1.87 us
  other arithmetic: 6.11 us -> 0 us
    pallas_call x0 -> x1, Pallas kernels: none -> 110 us  [on_device(): pl.pallas_call(functools.partial(kernel, n_ctx, n_head, heads), out_shape...]
    all_to_all x4 -> x0, waiting for transfers between devices: 59.3 us -> none  [the longest x1 30 us: fetch_picked(): lax.all_to_all(send_keys, 'ctx', split_axis=1, concat_axis=1, tiled=True)]
    all_gather x1 -> x0, blocking collectives: 48.3 us -> none  [on_device(): chosen = lax.all_gather(selected, 'ctx', axis=0, tiled=True)]
    dot_general x32 -> x0, matrix products: 32.8 us -> none  [the longest x8 14.4 us: on_device(): lax.dot_general(query_rows, key_rows, (((1,), (1,)), ((), ())), preferred...]
    all_to_all x4 -> x0, starting transfers between devices: 32.8 us -> none  [the longest x1 15 us: on_device(): lax.all_to_all(local_values, 'ctx', split_axis=1, concat_axis=0, tiled=True)]
    all_to_all x1 -> x0, blocking collectives: 24.5 us -> none  [on_device(): lax.all_to_all(block_rows, 'head', split_axis=0, concat_axis=1, tiled=True)]
    reshape x4 -> x0, local copies, waits for them, and re-layouts: 7.63 us -> none  [the longest x1 2.35 us: on_device(): picked_keys = picked_keys.reshape(blocks_here, TOPK, BLOCK, feat_width)]
    gather x2 -> x0, local copies, waits for them, and re-layouts: 5.08 us -> none  [the longest x1 3.16 us: fetch_picked(): send_keys = jnp.take(spread_keys, want_index, axis=0)]
  transfers between devices with their start and end apart: 4 -> 0, of which waited for: 3 -> 0; matrix products, arithmetic and copies ran while one was open for 17% -> 0% of each run, Pallas kernels for 0% -> 0%
where the time goes in v1:
time: 112 us
  Pallas kernels  110 us (98%)
  local copies, waits for them, and re-layouts  1.87 us (2%)
    pallas_call x1, Pallas kernels, on_device(): pl.pallas_call(functools.partial(kernel, n_ctx, n_head, heads), out_shape...  110 us

profile of v1, /device:TPU:1, one launch (start us, length us, event | category | flops | bytes accessed | tf_op | source)
XLA Modules:
  0.0 112.0 jit_solution(9055556311755440712)
XLA Ops:
  0.0 110.1 %moba.1 = bf16[32,8192]{1,0:T(8,128)(2,1)} custom-call(s32[1,3]{1,0:T(1,128)} %sel_ref.1, bf16[256,8,128]{2,1,0:T(8,128)(2,1)} %q_hbm.1, bf16[256,8,128]{2,1,0:T(8,128)(2,1)} %k_hbm.1, bf16[256,8,128]{2,1,0:T(8,128)(2,1)} %v_hbm.1), custom_call_target="tpu_custom_call" | custom-call | tf_op jit(solution)/shard_map/moba/pallas_call | solution.py:236
  110.1 1.9 %copy.6 = bf16[32,8192]{1,0:T(8,128)(2,1)} copy(bf16[32,8192]{1,0:T(8,128)(2,1)} %moba.1) | data formatting | bytes 1048576

commit v2 on v1

--- a/solution.py
+++ b/solution.py
@@ -10,7 +10,9 @@
 
 HEAD_DIM = 128
 BLOCK = 256
-CHUNKS = 2
+CHUNKS = 4
+QUERIES_AFTER = 1
+ATTEND_AFTER = 1
 MESH = pl.DeviceIdType.MESH
 STRIDE = 27
 
@@ -21,17 +23,18 @@
 def kernel(
     n_ctx, n_head, heads,
     sel_ref, q_hbm, k_hbm, v_hbm, out_ref,
-    q_ref, k_ref, v_ref, in_sem, q_heads, own, send, far, near, staged, wide,
+    q_ref, k_ref, v_ref, in_sem, q_heads, own, send, far, staged, wide,
+    q_next, part, part_back, stats, stats_back,
     sel_own, sel_all, sel_smem,
     sel_send, sel_recv, sel_local, spread_send, spread_recv, fetch_send, fetch_recv,
-    near_send, near_recv, out_send, out_recv,
+    back_send, back_recv, out_send, out_recv,
     *spread,
 ):
     group = heads // CHUNKS
     pieces_of_head = n_ctx // (2 * group)
     me = lax.axis_index("ctx")
     my_head = lax.axis_index("head")
-    right = lax.rem(me + 1, n_ctx)
+    right, left = lax.rem(me + 1, n_ctx), lax.rem(me + n_ctx - 1, n_ctx)
     rows_out = BLOCK // n_head
     cols_out = group * HEAD_DIM
 
@@ -88,12 +91,15 @@
             device_id={"ctx": peer}, device_id_type=MESH,
         )
 
-    def near_copy(chunk):
-        return pltpu.make_async_remote_copy(
-            src_ref=own.at[chunk], dst_ref=near.at[chunk],
-            send_sem=near_send.at[chunk], recv_sem=near_recv.at[chunk],
-            device_id={"ctx": right}, device_id_type=MESH,
-        )
+    def pass_copy(at, src, dst, peer):
+        return pltpu.make_async_remote_copy(
+            src_ref=src, dst_ref=dst, send_sem=back_send.at[at], recv_sem=back_recv.at[at],
+            device_id={"ctx": peer}, device_id_type=MESH,
+        )
+
+    query_copy = pass_copy(0, q_heads, q_next, left)
+    part_copy = pass_copy(1, part, part_back, right)
+    stats_copy = pass_copy(2, stats, stats_back, right)
 
     def sel_copy(peer):
         return pltpu.make_async_remote_copy(
@@ -127,6 +133,9 @@
     loads[1].wait()
     split_heads(v_ref, store_own(1), 0, heads)
 
+    loads[2].wait()
+    split_heads(q_ref, store_q, 0, heads)
+
     pl.semaphore_wait(barrier, n_ctx - 1 + n_head - 1)
 
     pltpu.make_async_copy(sel_own, sel_all.at[me], sel_recv).start()
@@ -142,15 +151,46 @@
         def _(i):
             spread_copy(chunk, to_ctx(i)).start()
 
-        near_copy(chunk).start()
-
-    loads[2].wait()
-    split_heads(q_ref, store_q, 0, heads)
+        if chunk == QUERIES_AFTER:
+            query_copy.start()
+
 
     wait_bytes(sel_all, sel_recv)
     sel_down = pltpu.make_async_copy(sel_all, sel_smem, sel_local)
     sel_down.start()
     sel_down.wait()
+
+    causal = lax.broadcasted_iota(jnp.int32, (BLOCK, BLOCK), 1) <= lax.broadcasted_iota(
+        jnp.int32, (BLOCK, BLOCK), 0
+    )
+    near_live, a_live, b_live = me >= 1, far_a != me, far_b != me
+    stat_lane = lax.broadcasted_iota(jnp.int32, (BLOCK, 128), 1)
+
+    def scores(q, k):
+        return lax.dot_general(q, k, (((1,), (1,)), ((), ())), preferred_element_type=jnp.float32)
+
+    def half_max(s):
+        return jnp.maximum(s[:, :128], s[:, 128:])
+
+    def pick(buf, kind, at):
+        first = (kind * group + at) * pieces_of_head
+        return buf[pl.ds(first, pieces_of_head)].reshape(BLOCK, HEAD_DIM)
+
+    def attend_next():
+        columns = jnp.zeros((BLOCK, 128), jnp.float32)
+        for h in range(heads):
+            chunk, at = divmod(h, group)
+            s = scores(q_next[h], pick(own.at[chunk], 0, at))
+            top = jnp.max(half_max(s), axis=1, keepdims=True) * EXP_SCALE
+            w = jnp.exp2(s * EXP_SCALE - top)
+            total = jnp.sum(w[:, :128] + w[:, 128:], axis=1, keepdims=True)
+            mixed = jnp.dot(
+                w.astype(jnp.bfloat16), pick(own.at[chunk], 1, at), preferred_element_type=jnp.float32
+            )
+            part[h] = (mixed / total).astype(jnp.bfloat16)
+            columns = jnp.where(stat_lane == 2 * h, top, columns)
+            columns = jnp.where(stat_lane == 2 * h + 1, total, columns)
+        stats[...] = columns.T[: 2 * heads]
 
     for chunk in range(CHUNKS):
         wait_bytes(spread[chunk], spread_recv.at[chunk])
@@ -168,44 +208,43 @@
         fill(me)
         pltpu.make_async_copy(send.at[chunk, me], far.at[chunk, :, me], fetch_recv.at[chunk]).start()
 
-    causal = lax.broadcasted_iota(jnp.int32, (BLOCK, BLOCK), 1) <= lax.broadcasted_iota(
-        jnp.int32, (BLOCK, BLOCK), 0
-    )
-    near_live, a_live, b_live = me >= 1, far_a != me, far_b != me
-
-    def scores(q, k):
-        return lax.dot_general(q, k, (((1,), (1,)), ((), ())), preferred_element_type=jnp.float32)
-
-    def half_max(s):
-        return jnp.maximum(s[:, :128], s[:, 128:])
+        if chunk == ATTEND_AFTER:
+            query_copy.wait_recv()
+            attend_next()
+            part_copy.start()
+            stats_copy.start()
+
+    part_copy.wait_recv()
+    stats_copy.wait_recv()
+    columns = jnp.concatenate(
+        [stats_back[...], jnp.zeros((128 - 2 * heads, BLOCK), jnp.float32)], 0
+    ).T
 
     for chunk in range(CHUNKS):
-        wait_bytes(near.at[chunk], near_recv.at[chunk])
         wait_bytes(far.at[chunk], fetch_recv.at[chunk])
 
         for at in range(group):
-            def pick(buf, kind):
-                first = (kind * group + at) * pieces_of_head
-                return buf[pl.ds(first, pieces_of_head)].reshape(BLOCK, HEAD_DIM)
-
-            blocks = [own.at[chunk], near.at[chunk], far.at[chunk, 0], far.at[chunk, 1]]
-            live = [None, near_live, a_live, b_live]
-            q = q_heads[chunk * group + at]
-            s = [scores(q, pick(b, 0)) for b in blocks]
+            blocks = [own.at[chunk], far.at[chunk, 0], far.at[chunk, 1]]
+            live = [None, a_live, b_live]
+            h = chunk * group + at
+            s = [scores(q_heads[h], pick(b, 0, at)) for b in blocks]
             s[0] = jnp.where(causal, s[0], FILL)
             top = half_max(s[0])
             for one, ok in zip(s[1:], live[1:]):
                 top = jnp.maximum(top, jnp.where(ok, half_max(one), FILL))
-            top = jnp.max(top, axis=1, keepdims=True) * EXP_SCALE
+            near_top = jnp.where(near_live, columns[:, 2 * h : 2 * h + 1], FILL)
+            top = jnp.maximum(jnp.max(top, axis=1, keepdims=True) * EXP_SCALE, near_top)
             total, mixed = None, None
             for one, ok, b in zip(s, live, blocks):
                 shift = top if ok is None else jnp.where(ok, top, -FILL)
                 w = jnp.exp2(one * EXP_SCALE - shift)
                 part = w[:, :128] + w[:, 128:]
                 total = part if total is None else total + part
-                part = jnp.dot(w.astype(jnp.bfloat16), pick(b, 1), preferred_element_type=jnp.float32)
+                part = jnp.dot(w.astype(jnp.bfloat16), pick(b, 1, at), preferred_element_type=jnp.float32)
                 mixed = part if mixed is None else mixed + part
-            total = jnp.sum(total, axis=1, keepdims=True)
+            near_total = jnp.exp2(near_top - top) * columns[:, 2 * h + 1 : 2 * h + 2]
+            total = jnp.sum(total, axis=1, keepdims=True) + near_total
+            mixed = mixed + part_back[h].astype(jnp.float32) * near_total
             rows = (mixed / total).astype(jnp.bfloat16)
             staged[chunk, :, :, at * HEAD_DIM : (at + 1) * HEAD_DIM] = rows.reshape(
                 n_head, rows_out, HEAD_DIM
@@ -219,10 +258,12 @@
 
     others = pl.ds(0, n_ctx - 1)
     wait_bytes(sel_all.at[others], sel_send)
+    query_copy.wait_send()
+    part_copy.wait_send()
+    stats_copy.wait_send()
     for chunk in range(CHUNKS):
         wait_bytes(spread[chunk].at[others], spread_send.at[chunk])
         wait_bytes(send.at[chunk, others], fetch_send.at[chunk])
-        wait_bytes(near.at[chunk], near_send.at[chunk])
         wait_bytes(staged.at[chunk, pl.ds(0, n_head - 1)], out_send.at[chunk])
         wait_bytes(staged.at[chunk], out_recv.at[chunk])
 
@@ -245,16 +286,17 @@
             pltpu.VMEM((CHUNKS, n_ctx, piece, HEAD_DIM), bf16),
             pltpu.VMEM((CHUNKS, n_ctx, 2, piece, HEAD_DIM), bf16),
             pltpu.VMEM((CHUNKS, 2, n_ctx, piece, HEAD_DIM), bf16),
-            pltpu.VMEM((CHUNKS, n_ctx, piece, HEAD_DIM), bf16),
             pltpu.VMEM((CHUNKS, n_head, BLOCK // n_head, group * HEAD_DIM), bf16),
             pltpu.VMEM((BLOCK * heads, HEAD_DIM), jnp.float32),
+            *[pltpu.VMEM((heads, BLOCK, HEAD_DIM), bf16)] * 3,
+            *[pltpu.VMEM((2 * heads, BLOCK), jnp.float32)] * 2,
             pltpu.VMEM((1, 128), jnp.int32),
             pltpu.VMEM((n_ctx, 1, 128), jnp.int32),
             pltpu.SMEM((n_ctx, 1, 128), jnp.int32),
             dma, dma, dma,
             dma((CHUNKS,)), dma((CHUNKS,)),
             dma((CHUNKS,)), dma((CHUNKS,)),
-            dma((CHUNKS,)), dma((CHUNKS,)),
+            dma((3,)), dma((3,)),
             dma((CHUNKS,)), dma((CHUNKS,)),
             *[pltpu.VMEM((n_ctx, piece, HEAD_DIM), bf16)] * CHUNKS,
         ],

time: 112 us -> 104 us (0.929)
  Pallas kernels: 110 us -> 101 us
    pallas_call x1, Pallas kernels: 110 us -> 101 us  [on_device(): pl.pallas_call(functools.partial(kernel, n_ctx, n_head, heads), out_shape...]
where the time goes in v2:
time: 104 us; the launch traced here: 103 us
  Pallas kernels  101 us (97%)
  local copies, waits for them, and re-layouts  1.87 us (2%)
    pallas_call x1, Pallas kernels, on_device(): pl.pallas_call(functools.partial(kernel, n_ctx, n_head, heads), out_shape...  101 us

profile of v2, /device:TPU:1, one launch (start us, length us, event | category | flops | bytes accessed | tf_op | source)
XLA Modules:
  0.0 103.0 jit_solution(15124979985123509587)
XLA Ops:
  0.0 101.1 %moba.1 = bf16[32,8192]{1,0:T(8,128)(2,1)} custom-call(s32[1,3]{1,0:T(1,128)} %sel_ref.1, bf16[256,8,128]{2,1,0:T(8,128)(2,1)} %q_hbm.1, bf16[256,8,128]{2,1,0:T(8,128)(2,1)} %k_hbm.1, bf16[256,8,128]{2,1,0:T(8,128)(2,1)} %v_hbm.1), custom_call_target="tpu_custom_call" | custom-call | tf_op jit(solution)/shard_map/moba/pallas_call | solution.py:277
  101.1 1.9 %copy.6 = bf16[32,8192]{1,0:T(8,128)(2,1)} copy(bf16[32,8192]{1,0:T(8,128)(2,1)} %moba.1) | data formatting | bytes 1048576

commit v3 on v2

--- a/solution.py
+++ b/solution.py
@@ -140,16 +140,17 @@
 
     pltpu.make_async_copy(sel_own, sel_all.at[me], sel_recv).start()
 
-    @pl.loop(1, n_ctx)
-    def _(i):
-        sel_copy(to_ctx(i)).start()
-
     for chunk in range(CHUNKS):
         pltpu.make_async_copy(own.at[chunk, me], spread[chunk].at[me], spread_recv.at[chunk]).start()
 
         @pl.loop(1, n_ctx)
         def _(i):
             spread_copy(chunk, to_ctx(i)).start()
+
+        if chunk == 0:
+            @pl.loop(1, n_ctx)
+            def _(i):
+                sel_copy(to_ctx(i)).start()
 
         if chunk == QUERIES_AFTER:
             query_copy.start()
@@ -195,17 +196,15 @@
     for chunk in range(CHUNKS):
         wait_bytes(spread[chunk], spread_recv.at[chunk])
 
-        def fill(peer):
+        @pl.loop(0, n_ctx, unroll=8)
+        def _(peer):
             for slot in range(2):
                 send[chunk, peer, slot] = spread[chunk][sel_smem[peer, 0, slot]]
 
         @pl.loop(1, n_ctx)
         def _(i):
-            peer = to_ctx(i)
-            fill(peer)
-            fetch_copy(chunk, peer).start()
-
-        fill(me)
+            fetch_copy(chunk, to_ctx(i)).start()
+
         pltpu.make_async_copy(send.at[chunk, me], far.at[chunk, :, me], fetch_recv.at[chunk]).start()
 
         if chunk == ATTEND_AFTER:

time: 104 us -> 104 us (level)
  no operation moved by 1% of the time
where the time goes in v3:
time: 104 us; the launch traced here: 103 us
  Pallas kernels  101 us (97%)
  local copies, waits for them, and re-layouts  1.87 us (2%)
    pallas_call x1, Pallas kernels, on_device(): pl.pallas_call(functools.partial(kernel, n_ctx, n_head, heads), out_shape...  101 us

profile of v3, /device:TPU:1, one launch (start us, length us, event | category | flops | bytes accessed | tf_op | source)
XLA Modules:
  0.0 102.6 jit_solution(11080807808985387726)
XLA Ops:
  0.0 100.7 %moba.1 = bf16[32,8192]{1,0:T(8,128)(2,1)} custom-call(s32[1,3]{1,0:T(1,128)} %sel_ref.1, bf16[256,8,128]{2,1,0:T(8,128)(2,1)} %q_hbm.1, bf16[256,8,128]{2,1,0:T(8,128)(2,1)} %k_hbm.1, bf16[256,8,128]{2,1,0:T(8,128)(2,1)} %v_hbm.1), custom_call_target="tpu_custom_call" | custom-call | tf_op jit(solution)/shard_map/moba/pallas_call | solution.py:276
  100.7 1.9 %copy.6 = bf16[32,8192]{1,0:T(8,128)(2,1)} copy(bf16[32,8192]{1,0:T(8,128)(2,1)} %moba.1) | data formatting | bytes 1048576

commit v4 on v2

--- a/solution.py
+++ b/solution.py
@@ -110,7 +110,7 @@
 
     def fetch_copy(chunk, peer):
         return pltpu.make_async_remote_copy(
-            src_ref=send.at[chunk, peer], dst_ref=far.at[chunk, :, me],
+            src_ref=send.at[chunk, peer], dst_ref=far.at[chunk, me],
             send_sem=fetch_send.at[chunk], recv_sem=fetch_recv.at[chunk],
             device_id={"ctx": peer}, device_id_type=MESH,
         )
@@ -206,7 +206,7 @@
             fetch_copy(chunk, peer).start()
 
         fill(me)
-        pltpu.make_async_copy(send.at[chunk, me], far.at[chunk, :, me], fetch_recv.at[chunk]).start()
+        pltpu.make_async_copy(send.at[chunk, me], far.at[chunk, me], fetch_recv.at[chunk]).start()
 
         if chunk == ATTEND_AFTER:
             query_copy.wait_recv()
@@ -224,7 +224,7 @@
         wait_bytes(far.at[chunk], fetch_recv.at[chunk])
 
         for at in range(group):
-            blocks = [own.at[chunk], far.at[chunk, 0], far.at[chunk, 1]]
+            blocks = [own.at[chunk], far.at[chunk, :, 0], far.at[chunk, :, 1]]
             live = [None, a_live, b_live]
             h = chunk * group + at
             s = [scores(q_heads[h], pick(b, 0, at)) for b in blocks]
@@ -285,7 +285,7 @@
             pltpu.VMEM((heads, BLOCK, HEAD_DIM), bf16),
             pltpu.VMEM((CHUNKS, n_ctx, piece, HEAD_DIM), bf16),
             pltpu.VMEM((CHUNKS, n_ctx, 2, piece, HEAD_DIM), bf16),
-            pltpu.VMEM((CHUNKS, 2, n_ctx, piece, HEAD_DIM), bf16),
+            pltpu.VMEM((CHUNKS, n_ctx, 2, piece, HEAD_DIM), bf16),
             pltpu.VMEM((CHUNKS, n_head, BLOCK // n_head, group * HEAD_DIM), bf16),
             pltpu.VMEM((BLOCK * heads, HEAD_DIM), jnp.float32),
             *[pltpu.VMEM((heads, BLOCK, HEAD_DIM), bf16)] * 3,

time: 104 us -> 104 us (level)
  no operation moved by 1% of the time
where the time goes in v4:
time: 104 us; the launch traced here: 103 us
  Pallas kernels  101 us (97%)
  local copies, waits for them, and re-layouts  1.87 us (2%)
    pallas_call x1, Pallas kernels, on_device(): pl.pallas_call(functools.partial(kernel, n_ctx, n_head, heads), out_shape...  101 us

profile of v4, /device:TPU:1, one launch (start us, length us, event | category | flops | bytes accessed | tf_op | source)
XLA Modules:
  0.0 103.0 jit_solution(14274273093708281301)
XLA Ops:
  0.0 101.1 %moba.1 = bf16[32,8192]{1,0:T(8,128)(2,1)} custom-call(s32[1,3]{1,0:T(1,128)} %sel_ref.1, bf16[256,8,128]{2,1,0:T(8,128)(2,1)} %q_hbm.1, bf16[256,8,128]{2,1,0:T(8,128)(2,1)} %k_hbm.1, bf16[256,8,128]{2,1,0:T(8,128)(2,1)} %v_hbm.1), custom_call_target="tpu_custom_call" | custom-call | tf_op jit(solution)/shard_map/moba/pallas_call | solution.py:277
  101.1 1.9 %copy.6 = bf16[32,8192]{1,0:T(8,128)(2,1)} copy(bf16[32,8192]{1,0:T(8,128)(2,1)} %moba.1) | data formatting | bytes 1048576
